TPU v7x, 32 devices: a whole 2x2x4 slice. The times are simulated.
32 devices in a mesh: rep: 1, exp: 32 (over z, y, x, core).
Axes of the slice: x: 2, y: 2, z: 4, core: 2. Of those that a mesh axis runs over, the one named last changes fastest.
Arguments:
- hidden: bfloat16 [512, 7168], P(('rep', 'exp')), may hold values from -6 to 6
- expert_ids: int32 [512, 8], P(('rep', 'exp')), may hold values from 0 to 15, all different within a row; in each aligned block of 16 rows (0 to 15, 16 to 31, ...) at most 10 rows name the same one
- router: bfloat16 [7168, 16], replicated, may hold values from -0.0625 to 0.0625
- gate_up: bfloat16 [32, 512, 2, 7168], P('exp', 'rep'), may hold values from -0.0625 to 0.0625
- down_weight: bfloat16 [32, 512, 7168], P('exp', 'rep'), may hold values from -0.1875 to 0.1875
- query_latent: bfloat16 [512, 64, 512], P(('rep', 'exp')), may hold values from -110 to 110
- query_rope: bfloat16 [512, 64, 64], P(('rep', 'exp')), may hold values from -6 to 6
- cache_latent: bfloat16 [512, 256, 512], P(('rep', 'exp')), may hold values from -8 to 8
- cache_rope: bfloat16 [512, 64, 256], P(('rep', 'exp')), may hold values from -5 to 5
- lengths: int32 [512], P(('rep', 'exp')), may hold values from 32 to 256, as said below
Outputs:
- moe_out: bfloat16 [512, 7168], P(('rep', 'exp'))
- attn_latent: bfloat16 [512, 64, 512], P(('rep', 'exp'))
Inputs may be any that keep to these rules, and one draw needn't show every extreme that they name: `expert_ids`: in every aligned block of 16 rows no expert is named by more than 10 pairs, a bound that some block reaches. `lengths`: some row has length 256.
All inputs are finite; a program needn't handle non-finite values.
Results may differ from a plain program's by a relative error of at most 0.015.
Values may be sent and summed in bfloat16 or wider, within the bound.
A program may use at most 128 MiB of HBM per device.

v0:
```python
import math

import jax
import jax.numpy as jnp
from jax import lax
from jax.sharding import PartitionSpec as P

ROPE = 64
NOPE = 128


route_scale = 2.827


def slot_table(expert_ids, experts, capacity):
    flat_ids = expert_ids.reshape(-1)
    onehot = (flat_ids[:, None] == jnp.arange(experts, dtype=jnp.int32)[None, :]).astype(jnp.int32)
    earlier = jnp.cumsum(onehot, axis=0) - onehot
    slot_rank = jnp.sum(earlier * onehot, axis=1)
    return flat_ids * capacity + slot_rank


def bucket_rows(rows_in, flat_slot, experts, capacity):
    row_total = rows_in.shape[0]
    pair_total = flat_slot.shape[0]
    slot_matrix = (
        jnp.arange(experts * capacity, dtype=jnp.int32)[:, None] == flat_slot[None, :]
    ).astype(jnp.float32)
    slot_matrix = jnp.sum(
        slot_matrix.reshape(experts * capacity, row_total, pair_total // row_total), axis=2
    )
    return jnp.dot(
        slot_matrix.astype(jnp.bfloat16), rows_in, preferred_element_type=jnp.float32
    ).astype(jnp.bfloat16)


def partial_output(rows_in, gate_up, down_weight):
    dims = (((1,), (1,)), ((), ()))
    gate_value = lax.dot_general(
        rows_in, gate_up[:, 0, :], dims, preferred_element_type=jnp.float32
    )
    up_value = lax.dot_general(rows_in, gate_up[:, 1, :], dims, preferred_element_type=jnp.float32)
    activated = (jax.nn.silu(gate_value) * up_value).astype(jnp.bfloat16)
    return jnp.dot(activated, down_weight, preferred_element_type=jnp.float32)


def attend(query_latent, query_rope, cache_latent, cache_rope, row_lengths):
    score_scale = 1.0 / math.sqrt(NOPE + ROPE)
    scores = jnp.einsum(
        "rhc,rlc->rhl", query_latent, cache_latent, preferred_element_type=jnp.float32
    )
    scores = scores + jnp.einsum(
        "rhp,rpl->rhl", query_rope, cache_rope, preferred_element_type=jnp.float32
    )
    scores = scores * score_scale
    valid_mask = (
        jnp.arange(cache_latent.shape[1], dtype=jnp.int32)[None, None, :]
        < row_lengths[:, None, None]
    )
    scores = jnp.where(valid_mask, scores, -1e30)
    row_max = jnp.max(scores, axis=2, keepdims=True)
    weights_raw = jnp.where(valid_mask, jnp.exp(scores - row_max), 0.0)
    attn_probs = (weights_raw / jnp.sum(weights_raw, axis=2, keepdims=True)).astype(jnp.bfloat16)
    output = jnp.einsum(
        "rhl,rlc->rhc", attn_probs, cache_latent, preferred_element_type=jnp.float32
    )
    return output.astype(jnp.bfloat16)


def on_device(
    hidden,
    expert_ids,
    router,
    gate_up,
    down_weight,
    query_latent,
    query_rope,
    cache_latent,
    cache_rope,
    lengths,
):
    groups = lax.axis_size("exp")
    experts = groups // 2
    rows_dev = hidden.shape[0]
    top_k = expert_ids.shape[1]
    model_width = hidden.shape[1]
    capacity = min(rows_dev, max(2, rows_dev * top_k * 5 // (4 * experts)))
    full_gate_up, full_down = (
        lax.all_gather(gate_up, "rep", axis=1, tiled=True),
        lax.all_gather(down_weight, "rep", axis=1, tiled=True),
    )
    slice_gate_up = full_gate_up[0]
    slice_down = full_down[0]
    logits = jnp.dot(hidden, router, preferred_element_type=jnp.float32)
    onehot = (expert_ids[:, :, None] == jnp.arange(experts, dtype=jnp.int32)[None, None, :]).astype(
        jnp.float32
    )
    picked = jnp.sum(onehot * logits[:, None, :], axis=2)
    sigmoid_scores = jax.nn.sigmoid(picked)
    mixing = sigmoid_scores / jnp.sum(sigmoid_scores, axis=1, keepdims=True) * route_scale
    flat_slot = slot_table(expert_ids, experts, capacity)
    buckets = bucket_rows(hidden, flat_slot, experts, capacity).reshape(
        experts, capacity, model_width
    )
    outgoing = jnp.broadcast_to(buckets[:, None], (experts, 2, capacity, model_width)).reshape(
        groups, capacity, model_width
    )
    arrived = lax.all_to_all(outgoing, "exp", split_axis=0, concat_axis=0, tiled=True)
    item_total = arrived.shape[1]
    slice_parts = (
        partial_output(arrived.reshape(-1, model_width), slice_gate_up, slice_down)
        .astype(jnp.bfloat16)
        .reshape(groups, item_total, model_width)
    )
    returned = lax.all_to_all(slice_parts, "exp", split_axis=0, concat_axis=0, tiled=True)
    paired = returned.reshape(experts, 2, capacity, model_width).astype(jnp.float32)
    answers = (paired[:, 0] + paired[:, 1]).astype(jnp.bfloat16)
    flat_answers = answers.reshape(experts * capacity, model_width)
    chosen = jnp.take(flat_answers, flat_slot, axis=0).reshape(rows_dev, top_k, model_width)
    moe_out = jnp.sum(chosen.astype(jnp.float32) * mixing[:, :, None], axis=1).astype(jnp.bfloat16)
    attn_latent = attend(query_latent, query_rope, cache_latent, cache_rope, lengths)
    return (moe_out, attn_latent)


def solution(mesh):
    return jax.shard_map(
        on_device,
        mesh=mesh,
        in_specs=(
            P(("rep", "exp"), None),
            P(("rep", "exp"), None),
            P(),
            P("exp", "rep", None, None),
            P("exp", "rep", None),
            P(("rep", "exp"), None, None),
            P(("rep", "exp"), None, None),
            P(("rep", "exp"), None, None),
            P(("rep", "exp"), None, None),
            P(("rep", "exp")),
        ),
        out_specs=(P(("rep", "exp"), None), P(("rep", "exp"), None, None)),
        check_vma=False,
    )
```

profile of v0, /device:TPU:0, one launch (start us, length us, event | category | flops | bytes accessed | tf_op | source)
XLA Modules:
  0.0 414.4 jit_solution(16258531707141799528)
XLA Ops:
  0.6 0.8 copy.23
  2.3 1.7 convolution_convert_fusion.1
  4.0 2.7 broadcast_in_dim.48
  6.6 5.9 %broadcast_in_dim.49 = bf16[16,2,10,7168]{3,2,1,0:T(8,128)(2,1)} broadcast(bf16[16,10,7168]{2,1,0:T(8,128)(2,1)} %broadcast_in_dim.48), dimensions={0,2,3} | broadcast | bytes 6881280 | tf_op jit(solution)/shard_map/broadcast_in_dim | solution.py:105
  12.5 7.4 %all-to-all-start = ((bf16[32,10,7168]{2,1,0:T(8,128)(2,1)}), bf16[32,10,7168]{2,1,0:T(8,128)(2,1)}, u32[]{:S(2)}, u32[]{:S(2)}) async-start(bf16[32,10,7168]{2,1,0:T(8,128)(2,1)} %bitcast.56), calls=%async_computation | async-start | bytes 14680064 | tf_op jit(solution)/shard_map/all_to_all | solution.py:108
  20.0 15.6 %copy.32 = bf16[1,512,2,7168]{3,1,2,0:T(8,128)(2,1)} copy(bf16[1,512,2,7168]{3,2,1,0:T(2,128)(2,1)} %param.13) | data formatting | bytes 29360128 | tf_op args[3]
  35.6 147.5 %all-to-all-done = bf16[32,10,7168]{2,1,0:T(8,128)(2,1)} async-done(((bf16[32,10,7168]{2,1,0:T(8,128)(2,1)}), bf16[32,10,7168]{2,1,0:T(8,128)(2,1)}, u32[]{:S(2)}, u32[]{:S(2)}) %all-to-all-start) | async-done | bytes 4587552 | tf_op jit(solution)/shard_map/all_to_all | solution.py:108
  183.1 8.0 %reshape.135 = bf16[320,7168]{1,0:T(8,128)(2,1)} reshape(bf16[32,10,7168]{2,1,0:T(8,128)(2,1)} %all-to-all-done) | data formatting | bytes 9175040 | tf_op jit(solution)/shard_map/reshape | solution.py:111
  191.1 7.0 %fusion.4 = f32[320,512]{1,0:T(8,128)S(1)} fusion(bf16[320,7168]{1,0:T(8,128)(2,1)} %reshape.135, bf16[512,2,7168]{2,0,1:T(8,128)(2,1)} %bitcast.57), kind=kOutput, calls=%fused_computation.12 | convolution fusion | flops 2348810240 | bytes 12582912 | tf_op jit(solution)/shard_map/dot_general | solution.py:39
  198.1 13.6 %convolution_convert_fusion = bf16[320,7168]{1,0:T(8,128)(2,1)} fusion(bf16[1,512,7168]{2,1,0:T(8,128)(2,1)} %param.14, bf16[320,7168]{1,0:T(8,128)(2,1)} %reshape.135, bf16[512,2,7168]{2,0,1:T(8,128)(2,1)} %bitcast.58, f32[320,512]{1,0:T(8,128)S(1)} %fusion.4), kind=kOutput, calls=%fused_computation.3 | convolution fusion | flops 4700897280 | bytes 24510464 | tf_op jit(solution)/shard_map/dot_general | solution.py:44
  211.7 7.8 %reshape.136 = bf16[32,10,7168]{2,1,0:T(8,128)(2,1)} reshape(bf16[320,7168]{1,0:T(8,128)(2,1)} %convolution_convert_fusion) | data formatting | bytes 9175040 | tf_op jit(solution)/shard_map/reshape | solution.py:113
  219.6 4.0 all-to-all-start.1
  223.7 0.2 fusion.29
  223.9 0.2 select_reduce_fusion
  224.3 3.6 fusion.30
  227.9 0.3 fusion.10
  228.2 0.4 fusion.28
  228.6 5.1 %convolution_convert_fusion.2 = bf16[16,64,512]{2,1,0:T(8,128)(2,1)} fusion(bf16[16,256,512]{2,1,0:T(8,128)(2,1)} %param.17, f32[16,64]{1,0:T(8,128)S(1)} %fusion.28, f32[16,64,256]{2,1,0:T(8,128)S(1)} %fusion.10, pred[16,256]{1,0:T(8,128)(4,1)S(1)} %iota_compare_fusion.3), kind=kOutput, calls=%fused_computation.17 | convolution fusion | flops 270009600 | bytes 6299648 | tf_op jit(solution)/shard_map/rhl,rlc->rhc/dot_general | solution.py:64
  233.7 152.9 %all-to-all-done.1 = bf16[32,10,7168]{2,1,0:T(8,128)(2,1)} async-done(((bf16[32,10,7168]{2,1,0:T(8,128)(2,1)}), bf16[32,10,7168]{2,1,0:T(8,128)(2,1)}, u32[]{:S(2)}, u32[]{:S(2)}) %all-to-all-start.1) | async-done | bytes 4587552 | tf_op jit(solution)/shard_map/all_to_all | solution.py:115
  386.6 10.2 %convert.1 = f32[16,2,10,7168]{3,2,1,0:T(8,128)} convert(bf16[16,2,10,7168]{3,2,1,0:T(8,128)(2,1)} %bitcast.6) | non-fusion elementwise | flops 2293760 | bytes 13762560 | tf_op jit(solution)/shard_map/convert_element_type | solution.py:116
  396.8 7.9 %fusion.2 = bf16[16,1,10,7168]{3,2,0,1:T(8,128)(2,1)} fusion(f32[16,2,10,7168]{3,2,1,0:T(8,128)} %convert.1), kind=kLoop, calls=%fused_computation.7 | loop fusion | flops 2293760 | bytes 11468800 | tf_op jit(solution)/shard_map/convert_element_type | solution.py:117
  404.7 3.2 convert_element_type.54
  407.9 3.0 gather_fusion
  410.8 3.6 multiply_reduce_fusion
  (26 shorter events, 1.1 us)
Async XLA Ops:
  0.6 223.7 %copy-start = (bf16[16,64,512]{2,1,0:T(8,128)(2,1)S(1)}, bf16[16,64,512]{2,1,0:T(8,128)(2,1)}, u32[]{:S(2)}) copy-start(bf16[16,64,512]{2,1,0:T(8,128)(2,1)} %param.15) | copy-start | bytes 3145732
  12.5 170.5 %all-to-all-start = ((bf16[32,10,7168]{2,1,0:T(8,128)(2,1)}), bf16[32,10,7168]{2,1,0:T(8,128)(2,1)}, u32[]{:S(2)}, u32[]{:S(2)}) async-start(bf16[32,10,7168]{2,1,0:T(8,128)(2,1)} %bitcast.56), calls=%async_computation | async-start | bytes 14680064 | tf_op jit(solution)/shard_map/all_to_all | solution.py:108
  219.5 4.1 copy-start.1
  219.5 4.1 copy-start.4
  219.6 4.7 %copy-start.5 = (s32[16]{0:T(128)S(1)}, s32[16]{0:T(128)}, u32[]{:S(2)}) copy-start(s32[16]{0:T(128)} %param.19) | copy-start | bytes 196
  219.6 167.0 %all-to-all-start.1 = ((bf16[32,10,7168]{2,1,0:T(8,128)(2,1)}), bf16[32,10,7168]{2,1,0:T(8,128)(2,1)}, u32[]{:S(2)}, u32[]{:S(2)}) async-start(bf16[32,10,7168]{2,1,0:T(8,128)(2,1)} %reshape.136), calls=%async_computation.1 | async-start | bytes 14680064 | tf_op jit(solution)/shard_map/all_to_all | solution.py:115
  223.5 4.3 %copy-start.2 = (bf16[16,64,256]{2,1,0:T(8,128)(2,1)S(1)}, bf16[16,64,256]{2,1,0:T(8,128)(2,1)}, u32[]{:S(2)}) copy-start(bf16[16,64,256]{2,1,0:T(8,128)(2,1)} %param.18) | copy-start | bytes 1572868
  223.5 4.3 %copy-start.3 = (bf16[16,64,64]{2,1,0:T(8,128)(2,1)S(1)}, bf16[16,64,64]{2,1,0:T(8,128)(2,1)}, u32[]{:S(2)}) copy-start(bf16[16,64,64]{2,1,0:T(8,128)(2,1)} %param.16) | copy-start | bytes 393220
where the time goes:
time: 415 us; the launch traced here: 414 us
  waiting for transfers between devices  300 us (72%)
  local copies, waits for them, and re-layouts  47.3 us (11%)
  matrix products  31.5 us (8%)
  other arithmetic  23.1 us (6%)
  starting transfers between devices  11.4 us (3%)
    all_to_all x1, waiting for transfers between devices, on_device(): lax.all_to_all(slice_parts, 'exp', split_axis=0, concat_axis=0, tiled=True)  153 us
    all_to_all x1, waiting for transfers between devices, on_device(): lax.all_to_all(outgoing, 'exp', split_axis=0, concat_axis=0, tiled=True)  147 us
    unnamed x14, local copies, waits for them, and re-layouts  16.5 us
    dot_general x1, matrix products, partial_output(): return jnp.dot(activated, down_weight, preferred_element_type=jnp.float32)  13.6 us
    convert_element_type x1, other arithmetic, on_device(): returned.reshape(experts, 2, capacity, model_width).astype(jnp.float32)  10.2 us
    broadcast_in_dim x2, local copies, waits for them, and re-layouts, on_device(): jnp.broadcast_to(buckets[:, None], (experts, 2, capacity, model_width))  8.56 us
  transfers between devices with their start and end apart: 2, of which 2 were waited for; matrix products, arithmetic and copies ran while one was open for 6% of the time, Pallas kernels for 0%

commit v1 on v0

--- a/solution.py
+++ b/solution.py
@@ -10,28 +10,6 @@
 
 
 route_scale = 2.827
-
-
-def slot_table(expert_ids, experts, capacity):
-    flat_ids = expert_ids.reshape(-1)
-    onehot = (flat_ids[:, None] == jnp.arange(experts, dtype=jnp.int32)[None, :]).astype(jnp.int32)
-    earlier = jnp.cumsum(onehot, axis=0) - onehot
-    slot_rank = jnp.sum(earlier * onehot, axis=1)
-    return flat_ids * capacity + slot_rank
-
-
-def bucket_rows(rows_in, flat_slot, experts, capacity):
-    row_total = rows_in.shape[0]
-    pair_total = flat_slot.shape[0]
-    slot_matrix = (
-        jnp.arange(experts * capacity, dtype=jnp.int32)[:, None] == flat_slot[None, :]
-    ).astype(jnp.float32)
-    slot_matrix = jnp.sum(
-        slot_matrix.reshape(experts * capacity, row_total, pair_total // row_total), axis=2
-    )
-    return jnp.dot(
-        slot_matrix.astype(jnp.bfloat16), rows_in, preferred_element_type=jnp.float32
-    ).astype(jnp.bfloat16)
 
 
 def partial_output(rows_in, gate_up, down_weight):
@@ -81,10 +59,6 @@
 ):
     groups = lax.axis_size("exp")
     experts = groups // 2
-    rows_dev = hidden.shape[0]
-    top_k = expert_ids.shape[1]
-    model_width = hidden.shape[1]
-    capacity = min(rows_dev, max(2, rows_dev * top_k * 5 // (4 * experts)))
     full_gate_up, full_down = (
         lax.all_gather(gate_up, "rep", axis=1, tiled=True),
         lax.all_gather(down_weight, "rep", axis=1, tiled=True),
@@ -98,26 +72,19 @@
     picked = jnp.sum(onehot * logits[:, None, :], axis=2)
     sigmoid_scores = jax.nn.sigmoid(picked)
     mixing = sigmoid_scores / jnp.sum(sigmoid_scores, axis=1, keepdims=True) * route_scale
-    flat_slot = slot_table(expert_ids, experts, capacity)
-    buckets = bucket_rows(hidden, flat_slot, experts, capacity).reshape(
-        experts, capacity, model_width
+    dense_mixing = jnp.sum(onehot * mixing[:, :, None], axis=1)
+    all_hidden = lax.all_gather(hidden, "exp", axis=0, tiled=True)
+    all_mixing = lax.all_gather(dense_mixing, "exp", axis=0, tiled=True)
+    own_expert = lax.axis_index("exp") // 2
+    own_mixing = jnp.sum(
+        jnp.where(jnp.arange(experts)[None, :] == own_expert, all_mixing, 0.0),
+        axis=1,
+        keepdims=True,
     )
-    outgoing = jnp.broadcast_to(buckets[:, None], (experts, 2, capacity, model_width)).reshape(
-        groups, capacity, model_width
+    weighted = (partial_output(all_hidden, slice_gate_up, slice_down) * own_mixing).astype(
+        jnp.bfloat16
     )
-    arrived = lax.all_to_all(outgoing, "exp", split_axis=0, concat_axis=0, tiled=True)
-    item_total = arrived.shape[1]
-    slice_parts = (
-        partial_output(arrived.reshape(-1, model_width), slice_gate_up, slice_down)
-        .astype(jnp.bfloat16)
-        .reshape(groups, item_total, model_width)
-    )
-    returned = lax.all_to_all(slice_parts, "exp", split_axis=0, concat_axis=0, tiled=True)
-    paired = returned.reshape(experts, 2, capacity, model_width).astype(jnp.float32)
-    answers = (paired[:, 0] + paired[:, 1]).astype(jnp.bfloat16)
-    flat_answers = answers.reshape(experts * capacity, model_width)
-    chosen = jnp.take(flat_answers, flat_slot, axis=0).reshape(rows_dev, top_k, model_width)
-    moe_out = jnp.sum(chosen.astype(jnp.float32) * mixing[:, :, None], axis=1).astype(jnp.bfloat16)
+    moe_out = lax.psum_scatter(weighted, "exp", scatter_dimension=0, tiled=True)
     attn_latent = attend(query_latent, query_rope, cache_latent, cache_rope, lengths)
     return (moe_out, attn_latent)
 

time: 415 us -> 266 us (0.64)
  waiting for transfers between devices: 300 us -> 155 us
  blocking collectives: 0 us -> 44.4 us
  local copies, waits for them, and re-layouts: 47.3 us -> 16.8 us
  other arithmetic: 23.1 us -> 0.96 us
  between operations: 0.82 us -> 14.2 us
  starting transfers between devices: 11.4 us -> 0.08 us
    all_to_all x2 -> x0, waiting for transfers between devices: 300 us -> none  [the longest x1 153 us: on_device(): lax.all_to_all(slice_parts, 'exp', split_axis=0, concat_axis=0, tiled=True)]
    reduce_scatter x0 -> x1, waiting for transfers between devices: none -> 136 us  [on_device(): moe_out = lax.psum_scatter(weighted, 'exp', scatter_dimension=0, tiled=True)]
    all_gather x0 -> x1, blocking collectives: none -> 44.4 us  [on_device(): all_mixing = lax.all_gather(dense_mixing, 'exp', axis=0, tiled=True)]
    all_gather x0 -> x1, waiting for transfers between devices: none -> 18.6 us  [on_device(): all_hidden = lax.all_gather(hidden, 'exp', axis=0, tiled=True)]
    convert_element_type x3 -> x0, other arithmetic: 18.2 us -> none  [the longest x1 10.2 us: on_device(): returned.reshape(experts, 2, capacity, model_width).astype(jnp.float32)]
    reshape x3 -> x0, local copies, waits for them, and re-layouts: 15.9 us -> none  [the longest x1 8.02 us: on_device(): arrived.reshape(-1, model_width)]
    all_to_all x2 -> x0, starting transfers between devices: 11.4 us -> none  [the longest x1 7.41 us: on_device(): lax.all_to_all(outgoing, 'exp', split_axis=0, concat_axis=0, tiled=True)]
    broadcast_in_dim x2 -> x0, local copies, waits for them, and re-layouts: 8.56 us -> none  [on_device(): jnp.broadcast_to(buckets[:, None], (experts, 2, capacity, model_width))]
  transfers between devices with their start and end apart: 2 -> 2, of which waited for: 2 -> 2; matrix products, arithmetic and copies ran while one was open for 6% -> 10% of each run, Pallas kernels for 0% -> 0%
where the time goes in v1:
time: 266 us; the launch traced here: 265 us
  waiting for transfers between devices  155 us (58%)
  blocking collectives  44.4 us (17%)
  matrix products  34.2 us (13%)
  local copies, waits for them, and re-layouts  16.8 us (6%)
  between operations  14.2 us (5%)
    reduce_scatter x1, waiting for transfers between devices, on_device(): moe_out = lax.psum_scatter(weighted, 'exp', scatter_dimension=0, tiled=True)  136 us
    all_gather x1, blocking collectives, on_device(): all_mixing = lax.all_gather(dense_mixing, 'exp', axis=0, tiled=True)  44.4 us
    all_gather x1, waiting for transfers between devices, on_device(): all_hidden = lax.all_gather(hidden, 'exp', axis=0, tiled=True)  18.6 us
    unnamed x24, local copies, waits for them, and re-layouts  16.6 us
    dot_general x1, matrix products, partial_output(): return jnp.dot(activated, down_weight, preferred_element_type=jnp.float32)  9.23 us
    dot_general x1, matrix products, partial_output(): lax.dot_general(rows_in, gate_up[:, 0, :], dims, preferred_element_type=j...  8.66 us
    dot_general x1, matrix products, partial_output(): lax.dot_general(rows_in, gate_up[:, 1, :], dims, preferred_element_type=j...  7.14 us
  transfers between devices with their start and end apart: 2, of which 2 were waited for; matrix products, arithmetic and copies ran while one was open for 10% of the time, Pallas kernels for 0%

profile of v1, /device:TPU:0, one launch (start us, length us, event | category | flops | bytes accessed | tf_op | source)
XLA Modules:
  0.0 265.4 jit_solution(13255697241960515935)
XLA Ops:
  7.2 0.0 all-gather.2.cloned.1.call-start
  7.2 0.7 all-gather.2.cloned.1.call-update
  7.9 0.0 reduce-scatter.2.cloned.1.call-start
  8.0 15.7 %copy.26 = bf16[1,512,2,7168]{3,1,2,0:T(8,128)(2,1)} copy(bf16[1,512,2,7168]{3,2,1,0:T(2,128)(2,1)} %param.13) | data formatting | bytes 29360128 | tf_op args[3]
  23.7 0.1 copy.20
  23.8 0.2 fusion.15
  24.0 0.2 select_reduce_fusion.2
  24.1 0.1 copy.21
  24.3 0.1 copy.22
  24.3 0.1 select_reduce_fusion.1
  24.5 44.4 %all_gather.9 = f32[512,16]{1,0:T(8,128)S(1)} all-gather(f32[16,16]{1,0:T(8,128)S(1)} %select_reduce_fusion.1), channel_id=1, replica_groups=mesh['rep'=1,'exp'=32] {'exp'}, dimensions={0}, use_global_device_ids=true | all-gather | bytes 33792 | tf_op jit(solution)/shard_map/all_gather | solution.py:77
  68.9 0.1 select_reduce_fusion
  69.0 18.6 %all-gather.2.cloned.1.call-done = bf16[512,7168]{1,0:T(8,128)(2,1)} async-done(((bf16[16,7168]{1,0:T(8,128)(2,1)}), bf16[512,7168]{1,0:T(8,128)(2,1)}) %all-gather.2.cloned.1.call-update) | async-done | bytes 7340048 | tf_op jit(solution)/shard_map/all_gather | solution.py:76
  87.7 8.7 %fusion.2 = f32[512,512]{1,0:T(8,128)S(1)} fusion(bf16[512,7168]{1,0:T(8,128)(2,1)} %all-gather.2.cloned.1.call-done, bf16[512,2,7168]{2,0,1:T(8,128)(2,1)} %bitcast.28), kind=kOutput, calls=%fused_computation.6 | convolution fusion | flops 3758096384 | bytes 15728640 | tf_op jit(solution)/shard_map/dot_general | solution.py:17
  96.4 0.2 slice-done.3
  96.6 7.1 %fusion.10 = bf16[512,512]{1,0:T(8,128)(2,1)S(1)} fusion(bf16[512,7168]{1,0:T(8,128)(2,1)} %all-gather.2.cloned.1.call-done, bf16[512,2,7168]{2,0,1:T(8,128)(2,1)S(1)} %bitcast.31, f32[512,512]{1,0:T(8,128)S(1)} %fusion.2), kind=kOutput, calls=%fused_computation.16 | convolution fusion | flops 3759669248 | bytes 16252928 | tf_op jit(solution)/shard_map/dot_general | solution.py:20
  103.7 9.2 %multiply_convert_fusion = bf16[512,7168]{1,0:T(8,128)(2,1)} fusion(bf16[512,512]{1,0:T(8,128)(2,1)S(1)} %fusion.10, bf16[1,512,7168]{2,1,0:T(8,128)(2,1)} %param.14, f32[512]{0:T(512)S(1)} %select_reduce_fusion), kind=kOutput, calls=%fused_computation.2 | convolution fusion | flops 3765436416 | bytes 15206400 | tf_op jit(solution)/shard_map/dot_general | solution.py:22
  113.0 0.6 copy-done.6
  113.6 0.1 iota_compare_fusion.1
  113.7 3.6 %fusion.16 = f32[16,64,256]{2,1,0:T(8,128)S(1)} fusion(bf16[16,64,512]{2,1,0:T(8,128)(2,1)S(1)} %copy-done, bf16[16,256,512]{2,1,0:T(8,128)(2,1)} %param.17), kind=kOutput, calls=%fused_computation.32 | convolution fusion | flops 268435456 | bytes 6291456 | tf_op jit(solution)/shard_map/rhc,rlc->rhl/dot_general | solution.py:27
  117.3 0.3 fusion.9
  117.6 0.4 fusion.14
  118.0 5.1 %convolution_convert_fusion = bf16[16,64,512]{2,1,0:T(8,128)(2,1)} fusion(bf16[16,256,512]{2,1,0:T(8,128)(2,1)} %param.17, f32[16,64]{1,0:T(8,128)S(1)} %fusion.14, f32[16,64,256]{2,1,0:T(8,128)S(1)} %fusion.9, pred[16,256]{1,0:T(8,128)(4,1)S(1)} %iota_compare_fusion.1), kind=kOutput, calls=%fused_computation.9 | convolution fusion | flops 270009600 | bytes 6299648 | tf_op jit(solution)/shard_map/rhl,rlc->rhc/dot_general | solution.py:42
  123.1 135.5 %reduce-scatter.2.cloned.1.call-done = bf16[16,7168]{1,0:T(8,128)(2,1)} async-done(((bf16[512,7168]{1,0:T(8,128)(2,1)}), bf16[16,7168]{1,0:T(8,128)(2,1)}) %reduce-scatter.2.cloned.1.call-update) | async-done | bytes 229392 | tf_op jit(solution)/shard_map/reduce_scatter | solution.py:87
  (25 shorter events, 0.1 us)
Async XLA Ops:
  7.2 106.5 %copy-start = (bf16[16,64,512]{2,1,0:T(8,128)(2,1)S(1)}, bf16[16,64,512]{2,1,0:T(8,128)(2,1)}, u32[]{:S(2)}) copy-start(bf16[16,64,512]{2,1,0:T(8,128)(2,1)} %param.15) | copy-start | bytes 3145732
  7.2 80.5 %all-gather.2.cloned.1.call-start = ((), (), s32[]{:S(2)}) async-start(), calls=%async_computation.1 | async-start | bytes 7569408 | tf_op jit(solution)/shard_map/all_gather | solution.py:76
  7.9 250.7 %reduce-scatter.2.cloned.1.call-start = ((), (), s32[]{:S(2)}) async-start(), calls=%async_computation.2 | async-start | bytes 7569408 | tf_op jit(solution)/shard_map/reduce_scatter | solution.py:87
  8.0 15.7 %copy-start.5 = (s32[16,8]{0,1:T(8,128)S(1)}, s32[16,8]{0,1:T(8,128)}, u32[]{:S(2)}) copy-start(s32[16,8]{0,1:T(8,128)} %param.11) | copy-start | bytes 1540
  8.0 15.8 %copy-start.1 = (bf16[16,7168]{1,0:T(8,128)(2,1)S(1)}, bf16[16,7168]{1,0:T(8,128)(2,1)}, u32[]{:S(2)}) copy-start(bf16[16,7168]{1,0:T(8,128)(2,1)} %param.10) | copy-start | bytes 688132
  8.0 15.8 %copy-start.4 = (bf16[7168,16]{0,1:T(8,128)(2,1)S(1)}, bf16[7168,16]{0,1:T(8,128)(2,1)}, u32[]{:S(2)}) copy-start(bf16[7168,16]{0,1:T(8,128)(2,1)} %param.12) | copy-start | bytes 688132
  24.5 71.9 %slice-start = ((s8[14680064]{0:T(1024)(128)(4,1)}), s8[2097152]{0:T(1024)(128)(4,1)S(1)}, s32[]{:S(2)}) async-start(s8[14680064]{0:T(1024)(128)(4,1)} %bitcast.29), calls=%async_computation.3 | async-start | bytes 4194304
  87.7 8.7 %slice-start.1 = ((s8[14680064]{0:T(1024)(128)(4,1)}), s8[4194304]{0:T(1024)(128)(4,1)S(1)}, s32[]{:S(2)}) async-start(s8[14680064]{0:T(1024)(128)(4,1)} %bitcast.29), calls=%async_computation.4 | async-start | bytes 8388608
  87.7 8.7 %slice-start.2 = ((s8[14680064]{0:T(1024)(128)(4,1)}), s8[4194304]{0:T(1024)(128)(4,1)S(1)}, s32[]{:S(2)}) async-start(s8[14680064]{0:T(1024)(128)(4,1)} %bitcast.29), calls=%async_computation.5 | async-start | bytes 8388608
  87.7 8.9 %slice-start.3 = ((s8[14680064]{0:T(1024)(128)(4,1)}), s8[4194304]{0:T(1024)(128)(4,1)S(1)}, s32[]{:S(2)}) async-start(s8[14680064]{0:T(1024)(128)(4,1)} %bitcast.29), calls=%async_computation.6 | async-start | bytes 8388608
  112.9 0.7 copy-start.6
  112.9 4.3 %copy-start.2 = (bf16[16,64,256]{2,1,0:T(8,128)(2,1)S(1)}, bf16[16,64,256]{2,1,0:T(8,128)(2,1)}, u32[]{:S(2)}) copy-start(bf16[16,64,256]{2,1,0:T(8,128)(2,1)} %param.18) | copy-start | bytes 1572868
  113.0 4.3 %copy-start.3 = (bf16[16,64,64]{2,1,0:T(8,128)(2,1)S(1)}, bf16[16,64,64]{2,1,0:T(8,128)(2,1)}, u32[]{:S(2)}) copy-start(bf16[16,64,64]{2,1,0:T(8,128)(2,1)} %param.16) | copy-start | bytes 393220
Sparse Core Ops, SparseCore 0:
  10.8 76.7 all-gather.1
  113.1 145.4 reduce-scatter.1

commit v2 on v1

--- a/solution.py
+++ b/solution.py
@@ -3,6 +3,8 @@
 import jax
 import jax.numpy as jnp
 from jax import lax
+from jax.experimental import pallas as pl
+from jax.experimental.pallas import tpu as pltpu
 from jax.sharding import PartitionSpec as P
 
 ROPE = 64
@@ -12,14 +14,288 @@
 route_scale = 2.827
 
 
-def partial_output(rows_in, gate_up, down_weight):
-    dims = (((1,), (1,)), ((), ()))
-    gate_value = lax.dot_general(
-        rows_in, gate_up[:, 0, :], dims, preferred_element_type=jnp.float32
-    )
-    up_value = lax.dot_general(rows_in, gate_up[:, 1, :], dims, preferred_element_type=jnp.float32)
-    activated = (jax.nn.silu(gate_value) * up_value).astype(jnp.bfloat16)
-    return jnp.dot(activated, down_weight, preferred_element_type=jnp.float32)
+EXTRA = 128
+
+
+def other_z(z, dz):
+    return (z, z + 1 - 2 * (z % 2), z + 2 - 4 * (z // 2), 3 - z)[dz]
+
+
+def expert_kernel(
+    own_ref,
+    gate_up_hbm,
+    down_hbm,
+    out_ref,
+    rows_ref,
+    gate_up_ref,
+    down_ref,
+    part_ref,
+    from_core,
+    from_q,
+    from_p,
+    from_z,
+    gate_acc,
+    up_acc,
+    weight_sem,
+    ag_send,
+    ag_recv,
+    rs_send,
+    rs_recv,
+):
+    width = down_ref.shape[1]
+    tile = 1024
+    experts = 16
+    me = lax.axis_index("exp")
+    core, x, y, z = me % 2, (me // 2) % 2, (me // 4) % 2, me // 8
+    p_step, q_step = 4 - 2 * core, 2 + 2 * core
+    p_at = y * (1 - core) + x * core
+    q_at = x * (1 - core) + y * core
+
+    def device(zz, p, q, c):
+        return 8 * zz + p_step * p + q_step * q + c
+
+    sibling = device(z, p_at, q_at, 1 - core)
+    p_near = device(z, 1 - p_at, q_at, core)
+    q_near = device(z, p_at, 1 - q_at, core)
+    z_near = [device(other_z(z, dz), p_at, q_at, core) for dz in range(4)]
+
+    barrier = pltpu.get_barrier_semaphore()
+    for partner in (sibling, p_near, q_near, *z_near[1:]):
+        pl.semaphore_signal(
+            barrier, inc=1, device_id={"exp": partner}, device_id_type=pl.DeviceIdType.MESH
+        )
+    gate_up_copy = pltpu.make_async_copy(gate_up_hbm, gate_up_ref, weight_sem.at[0])
+    down_copy = pltpu.make_async_copy(down_hbm, down_ref, weight_sem.at[1])
+    gate_up_copy.start()
+    down_copy.start()
+    rows_ref[me] = own_ref[...]
+    pl.semaphore_wait(barrier, 6)
+
+    sent = []
+
+    def remote(src, dst, send, recv, target):
+        return pltpu.make_async_remote_copy(
+            src_ref=src,
+            dst_ref=dst,
+            send_sem=send,
+            recv_sem=recv,
+            device_id={"exp": target},
+            device_id_type=pl.DeviceIdType.MESH,
+        )
+
+    ag_count = [0]
+
+    def give(block, target):
+        copy = remote(
+            rows_ref.at[block],
+            rows_ref.at[block],
+            ag_send.at[ag_count[0]],
+            ag_recv.at[block],
+            target,
+        )
+        ag_count[0] += 1
+        copy.start()
+        sent.append(copy)
+
+    def take(block):
+        remote(
+            rows_ref.at[block], rows_ref.at[block], ag_send.at[0], ag_recv.at[block], sibling
+        ).wait_recv()
+
+    def gather_first(dz):
+        zz = other_z(z, dz)
+        block = device(zz, p_at, q_at, core)
+        if dz == 0:
+            for far in (1, 2, 3):
+                give(block, z_near[far])
+        else:
+            take(block)
+        give(block, q_near)
+        give(block, p_near)
+        give(block, sibling)
+
+    def gather_second(dz):
+        zz = other_z(z, dz)
+        block = device(zz, 1 - p_at, q_at, core)
+        take(block)
+        give(block, q_near)
+        give(block, sibling)
+
+    def gather_last(dz):
+        zz = other_z(z, dz)
+        for p in (p_at, 1 - p_at):
+            block = device(zz, p, 1 - q_at, core)
+            take(block)
+            give(block, sibling)
+        for p in (0, 1):
+            for q in (0, 1):
+                take(device(zz, p, q, 1 - core))
+
+    rs_count = [0]
+
+    def hand_over(block, slots, slot, recv, target):
+        copy = remote(
+            part_ref.at[block], slots.at[slot], rs_send.at[rs_count[0]], rs_recv.at[recv], target
+        )
+        rs_count[0] += 1
+        copy.start()
+        sent.append(copy)
+
+    def receive(slots, slot, recv):
+        remote(
+            slots.at[slot], slots.at[slot], rs_send.at[0], rs_recv.at[recv], sibling
+        ).wait_recv()
+
+    def add(block, slots, slot):
+        total = part_ref[block].astype(jnp.float32) + slots[slot].astype(jnp.float32)
+        part_ref[block] = total.astype(jnp.bfloat16)
+
+    def compute(dz):
+        zz = other_z(z, dz)
+        gate_acc[...] = jnp.zeros_like(gate_acc)
+        up_acc[...] = jnp.zeros_like(up_acc)
+        dims = (((1,), (1,)), ((), ()))
+        planes = pl.ds(8 * zz, 8)
+
+        @pl.loop(0, width // tile)
+        def _(step):
+            columns = pl.ds(pl.multiple_of(step * tile, tile), tile)
+            rows = rows_ref[planes, :, columns].reshape(128, tile)
+            gate_acc[...] += lax.dot_general(
+                rows, gate_up_ref[0, :, columns], dims, preferred_element_type=jnp.float32
+            )
+            up_acc[...] += lax.dot_general(
+                rows, gate_up_ref[1, :, columns], dims, preferred_element_type=jnp.float32
+            )
+
+        gate = gate_acc[...]
+        act = (gate / (1.0 + jnp.exp(-gate)) * up_acc[...]).astype(jnp.bfloat16)
+        extra = rows_ref[planes, :, width:].reshape(128, EXTRA).astype(jnp.float32)
+        lane = lax.broadcasted_iota(jnp.int32, (128, EXTRA), 1)
+        own = (lane == me // 2) | (lane == experts + me // 2)
+        mixing = jnp.sum(jnp.where(own, extra, 0.0), axis=1, keepdims=True)
+
+        if dz == 0:
+            down_copy.wait()
+
+        @pl.loop(0, width // tile)
+        def _(step):
+            columns = pl.ds(pl.multiple_of(step * tile, tile), tile)
+            result = jnp.dot(act, down_ref[:, columns], preferred_element_type=jnp.float32)
+            part_ref[planes, :, columns] = (
+                (result * mixing).astype(jnp.bfloat16).reshape(8, 16, tile)
+            )
+
+        for yy in (0, 1):
+            for xx in (0, 1):
+                block = 8 * zz + 4 * yy + 2 * xx + 1 - core
+                slot = 4 * dz + 2 * yy + xx
+                hand_over(block, from_core, slot, slot, sibling)
+
+    def sum_cores(dz):
+        zz = other_z(z, dz)
+        for q in (1 - q_at, q_at):
+            for i, p in enumerate((1 - p_at, p_at)):
+                slot = 4 * dz + (p_step // 2) * p + (q_step // 2) * q
+                block = device(zz, p, q, core)
+                receive(from_core, slot, slot)
+                add(block, from_core, slot)
+                if q is not q_at:
+                    hand_over(block, from_q, 2 * dz + i, 16 + 2 * dz + i, q_near)
+
+    def sum_q(dz):
+        zz = other_z(z, dz)
+        for i, p in enumerate((1 - p_at, p_at)):
+            block = device(zz, p, q_at, core)
+            receive(from_q, 2 * dz + i, 16 + 2 * dz + i)
+            add(block, from_q, 2 * dz + i)
+            if i == 0:
+                hand_over(block, from_p, dz, 24 + dz, p_near)
+
+    def sum_p(dz):
+        block = z_near[dz]
+        receive(from_p, dz, 24 + dz)
+        add(block, from_p, dz)
+        if dz:
+            hand_over(block, from_z, dz - 1, 27 + dz, z_near[dz])
+
+    gather_first(0)
+    gather_first(1)
+    gather_second(0)
+    gather_first(2)
+    gather_second(1)
+    gather_last(0)
+    gate_up_copy.wait()
+    compute(0)
+    gather_first(3)
+    gather_second(2)
+    gather_last(1)
+    sum_cores(0)
+    compute(1)
+    gather_second(3)
+    gather_last(2)
+    sum_cores(1)
+    sum_q(0)
+    compute(2)
+    gather_last(3)
+    sum_cores(2)
+    sum_q(1)
+    sum_p(0)
+    compute(3)
+    sum_cores(3)
+    sum_q(2)
+    sum_p(1)
+    sum_q(3)
+    sum_p(2)
+    sum_p(3)
+    total = part_ref[me].astype(jnp.float32)
+    for dz in (1, 2, 3):
+        receive(from_z, dz - 1, 27 + dz)
+        total = total + from_z[dz - 1].astype(jnp.float32)
+    out_ref[...] = total.astype(jnp.bfloat16)
+    for copy in sent:
+        copy.wait_send()
+
+
+def experts_layer(own, gate_up, down):
+    hidden_dev, width = down.shape
+    rows_dev = own.shape[0]
+    groups = lax.axis_size("exp")
+    block = (rows_dev, width)
+    flops = 2 * groups * rows_dev * width * hidden_dev * 3
+    return pl.pallas_call(
+        expert_kernel,
+        out_shape=jax.ShapeDtypeStruct(block, jnp.bfloat16),
+        in_specs=[
+            pl.BlockSpec(memory_space=pltpu.VMEM),
+            pl.BlockSpec(memory_space=pl.ANY),
+            pl.BlockSpec(memory_space=pl.ANY),
+        ],
+        out_specs=pl.BlockSpec(memory_space=pltpu.VMEM),
+        scratch_shapes=[
+            pltpu.VMEM((groups, rows_dev, width + EXTRA), jnp.bfloat16),
+            pltpu.VMEM((2, hidden_dev, width), jnp.bfloat16),
+            pltpu.VMEM((hidden_dev, width), jnp.bfloat16),
+            pltpu.VMEM((groups, *block), jnp.bfloat16),
+            pltpu.VMEM((16, *block), jnp.bfloat16),
+            pltpu.VMEM((8, *block), jnp.bfloat16),
+            pltpu.VMEM((4, *block), jnp.bfloat16),
+            pltpu.VMEM((3, *block), jnp.bfloat16),
+            pltpu.VMEM((8 * rows_dev, hidden_dev), jnp.float32),
+            pltpu.VMEM((8 * rows_dev, hidden_dev), jnp.float32),
+            pltpu.SemaphoreType.DMA((2,)),
+            pltpu.SemaphoreType.DMA((31,)),
+            pltpu.SemaphoreType.DMA((groups,)),
+            pltpu.SemaphoreType.DMA((31,)),
+            pltpu.SemaphoreType.DMA((31,)),
+        ],
+        compiler_params=pltpu.CompilerParams(
+            collective_id=0, has_side_effects=True, vmem_limit_bytes=56 * 2**20
+        ),
+        cost_estimate=pl.CostEstimate(
+            flops=flops, bytes_accessed=6 * hidden_dev * width, transcendentals=0
+        ),
+    )(own, gate_up, down)
 
 
 def attend(query_latent, query_rope, cache_latent, cache_rope, row_lengths):
@@ -73,18 +349,11 @@
     sigmoid_scores = jax.nn.sigmoid(picked)
     mixing = sigmoid_scores / jnp.sum(sigmoid_scores, axis=1, keepdims=True) * route_scale
     dense_mixing = jnp.sum(onehot * mixing[:, :, None], axis=1)
-    all_hidden = lax.all_gather(hidden, "exp", axis=0, tiled=True)
-    all_mixing = lax.all_gather(dense_mixing, "exp", axis=0, tiled=True)
-    own_expert = lax.axis_index("exp") // 2
-    own_mixing = jnp.sum(
-        jnp.where(jnp.arange(experts)[None, :] == own_expert, all_mixing, 0.0),
-        axis=1,
-        keepdims=True,
-    )
-    weighted = (partial_output(all_hidden, slice_gate_up, slice_down) * own_mixing).astype(
-        jnp.bfloat16
-    )
-    moe_out = lax.psum_scatter(weighted, "exp", scatter_dimension=0, tiled=True)
+    high = lax.reduce_precision(dense_mixing, 8, 7)
+    extra = jnp.concatenate((high, dense_mixing - high), axis=1)
+    extra = jnp.pad(extra, ((0, 0), (0, EXTRA - extra.shape[1]))).astype(jnp.bfloat16)
+    own = jnp.concatenate((hidden, extra), axis=1)
+    moe_out = experts_layer(own, slice_gate_up.transpose(1, 0, 2), slice_down)
     attn_latent = attend(query_latent, query_rope, cache_latent, cache_rope, lengths)
     return (moe_out, attn_latent)
 

time: 266 us -> 130 us (0.49)
  the two profiles are of different devices: /device:TPU:0 before, /device:TPU:17 now
where the time goes in v2:
time: 130 us; the launch traced here: 129 us
  Pallas kernels  101 us (78%)
  local copies, waits for them, and re-layouts  17.3 us (13%)
  matrix products  8.04 us (6%)
  other arithmetic  2.53 us (2%)
    pallas_call x1, Pallas kernels, experts_layer(): pl.pallas_call(expert_kernel, out_shape=jax.ShapeDtypeStruct(block, jnp.b...  101 us
    unnamed x15, local copies, waits for them, and re-layouts  17.2 us
    dot_general x1, matrix products, attend(): jnp.einsum('rhl,rlc->rhc', attn_probs, cache_latent, preferred_element_ty...  5.13 us

profile of v2, /device:TPU:17, one launch (start us, length us, event | category | flops | bytes accessed | tf_op | source)
XLA Modules:
  0.0 129.5 jit_solution(4842281342481638291)
XLA Ops:
  0.6 0.0 copy-start
  0.6 0.8 copy.17
  1.5 1.2 fusion.14
  2.7 0.2 select_reduce_fusion.1
  2.9 0.1 copy.18
  3.0 0.1 copy.19
  3.1 0.1 select_reduce_fusion
  3.3 0.1 fusion.10
  3.3 1.6 %pad_maximum_fusion.own_ref = bf16[16,7296]{1,0:T(8,128)(2,1)} fusion(bf16[16,128]{1,0:T(8,128)(2,1)S(1)} %fusion.10, bf16[16,7168]{1,0:T(8,128)(2,1)} %param.10), kind=kLoop, calls=%fused_computation.11 | loop fusion | flops 466944 | bytes 466944 | tf_op jit(solution)/shard_map/concatenate | solution.py:355
  5.0 15.6 %copy.22 = bf16[1,512,2,7168]{3,1,2,0:T(8,128)(2,1)} copy(bf16[1,512,2,7168]{3,2,1,0:T(2,128)(2,1)} %param.13) | data formatting | bytes 29360128 | tf_op args[3]
  20.6 100.8 %shard_map.113 = bf16[16,7168]{1,0:T(8,128)(2,1)} custom-call(bf16[16,7296]{1,0:T(8,128)(2,1)} %pad_maximum_fusion.own_ref, bf16[2,512,7168]{2,1,0:T(8,128)(2,1)} %bitcast.15, bf16[512,7168]{1,0:T(8,128)(2,1)} %bitcast.16), custom_call_target="tpu_custom_call" | custom-call | flops 11274289152 | bytes 22020096 | tf_op jit(solution)/shard_map/pallas_call | solution.py:266
  121.4 0.0 copy-done.5
  121.4 0.0 copy-start.2
  121.4 0.0 copy-start.3
  121.5 0.1 iota_compare_fusion.1
  121.5 0.0 copy-done
  121.5 1.4 %fusion.15 = f32[16,64,256]{2,1,0:T(8,128)S(1)} fusion(bf16[16,64,512]{2,1,0:T(8,128)(2,1)S(1)} %copy-done, bf16[16,256,512]{2,1,0:T(8,128)(2,1)S(1)} %copy-done.1), kind=kOutput, calls=%fused_computation.30 | convolution fusion | flops 268435456 | bytes 6291456 | tf_op jit(solution)/shard_map/rhc,rlc->rhl/dot_general | solution.py:303
  122.9 0.0 copy-done.2
  122.9 0.0 copy-done.3
  122.9 0.3 fusion.5
  123.2 0.4 fusion.13
  123.6 5.1 %convolution_convert_fusion = bf16[16,64,512]{2,1,0:T(8,128)(2,1)} fusion(bf16[16,256,512]{2,1,0:T(8,128)(2,1)} %param.17, f32[16,64]{1,0:T(8,128)S(1)} %fusion.13, f32[16,64,256]{2,1,0:T(8,128)S(1)} %fusion.5, pred[16,256]{1,0:T(8,128)(4,1)S(1)} %iota_compare_fusion.1), kind=kOutput, calls=%fused_computation.3 | convolution fusion | flops 270009600 | bytes 6299648 | tf_op jit(solution)/shard_map/rhl,rlc->rhc/dot_general | solution.py:318
  128.8 0.0 copy-done.4
  128.8 0.7 copy.24
  (7 shorter events, 0.1 us)
Async XLA Ops:
  0.6 120.9 %copy-start = (bf16[16,64,512]{2,1,0:T(8,128)(2,1)S(1)}, bf16[16,64,512]{2,1,0:T(8,128)(2,1)}, u32[]{:S(2)}) copy-start(bf16[16,64,512]{2,1,0:T(8,128)(2,1)} %param.15) | copy-start | bytes 3145732
  20.6 100.8 %copy-start.5 = (s32[16]{0:T(128)S(1)}, s32[16]{0:T(128)}, u32[]{:S(2)}) copy-start(s32[16]{0:T(128)} %param.19) | copy-start | bytes 196
  20.6 100.9 %copy-start.1 = (bf16[16,256,512]{2,1,0:T(8,128)(2,1)S(1)}, bf16[16,256,512]{2,1,0:T(8,128)(2,1)}, u32[]{:S(2)}) copy-start(bf16[16,256,512]{2,1,0:T(8,128)(2,1)} %param.17) | copy-start | bytes 12582916
  121.4 1.5 %copy-start.2 = (bf16[16,64,256]{2,1,0:T(8,128)(2,1)S(1)}, bf16[16,64,256]{2,1,0:T(8,128)(2,1)}, u32[]{:S(2)}) copy-start(bf16[16,64,256]{2,1,0:T(8,128)(2,1)} %param.18) | copy-start | bytes 1572868
  121.4 1.5 %copy-start.3 = (bf16[16,64,64]{2,1,0:T(8,128)(2,1)S(1)}, bf16[16,64,64]{2,1,0:T(8,128)(2,1)}, u32[]{:S(2)}) copy-start(bf16[16,64,64]{2,1,0:T(8,128)(2,1)} %param.16) | copy-start | bytes 393220
  123.6 5.1 %copy-start.4 = (bf16[16,7168]{1,0:T(8,128)(2,1)S(1)}, bf16[16,7168]{1,0:T(8,128)(2,1)}, u32[]{:S(2)}) copy-start(bf16[16,7168]{1,0:T(8,128)(2,1)} %shard_map.113) | copy-start | bytes 688132

commit v3 on v2

--- a/solution.py
+++ b/solution.py
@@ -22,10 +22,16 @@
 
 
 def expert_kernel(
+    lengths_ref,
     own_ref,
     gate_up_hbm,
     down_hbm,
+    query_latent_hbm,
+    query_rope_hbm,
+    cache_latent_hbm,
+    cache_rope_hbm,
     out_ref,
+    attn_ref,
     rows_ref,
     gate_up_ref,
     down_ref,
@@ -34,9 +40,14 @@
     from_q,
     from_p,
     from_z,
-    gate_acc,
-    up_acc,
+    acc,
+    select,
+    query_latent,
+    query_rope,
+    cache_latent,
+    cache_rope,
     weight_sem,
+    attn_sem,
     ag_send,
     ag_recv,
     rs_send,
@@ -64,7 +75,22 @@
         pl.semaphore_signal(
             barrier, inc=1, device_id={"exp": partner}, device_id_type=pl.DeviceIdType.MESH
         )
-    gate_up_copy = pltpu.make_async_copy(gate_up_hbm, gate_up_ref, weight_sem.at[0])
+    attn_copies = [
+        pltpu.make_async_copy(src, dst, attn_sem.at[i])
+        for i, (src, dst) in enumerate(
+            (
+                (query_latent_hbm, query_latent),
+                (query_rope_hbm, query_rope),
+                (cache_latent_hbm, cache_latent),
+                (cache_rope_hbm, cache_rope),
+            )
+        )
+    ]
+    for copy in attn_copies:
+        copy.start()
+    gate_up_copy = pltpu.make_async_copy(
+        gate_up_hbm.reshape(gate_up_ref.shape), gate_up_ref, weight_sem.at[0]
+    )
     down_copy = pltpu.make_async_copy(down_hbm, down_ref, weight_sem.at[1])
     gate_up_copy.start()
     down_copy.start()
@@ -152,8 +178,7 @@
 
     def compute(dz):
         zz = other_z(z, dz)
-        gate_acc[...] = jnp.zeros_like(gate_acc)
-        up_acc[...] = jnp.zeros_like(up_acc)
+        acc[...] = jnp.zeros_like(acc)
         dims = (((1,), (1,)), ((), ()))
         planes = pl.ds(8 * zz, 8)
 
@@ -161,15 +186,16 @@
         def _(step):
             columns = pl.ds(pl.multiple_of(step * tile, tile), tile)
             rows = rows_ref[planes, :, columns].reshape(128, tile)
-            gate_acc[...] += lax.dot_general(
-                rows, gate_up_ref[0, :, columns], dims, preferred_element_type=jnp.float32
-            )
-            up_acc[...] += lax.dot_general(
-                rows, gate_up_ref[1, :, columns], dims, preferred_element_type=jnp.float32
-            )
-
-        gate = gate_acc[...]
-        act = (gate / (1.0 + jnp.exp(-gate)) * up_acc[...]).astype(jnp.bfloat16)
+            acc[...] += lax.dot_general(
+                rows, gate_up_ref[:, columns], dims, preferred_element_type=jnp.float32
+            )
+
+        gate = acc[...]
+        up = pltpu.roll(gate, gate.shape[1] - 1, 1)
+        even = lax.broadcasted_iota(jnp.int32, gate.shape, 1) % 2 == 0
+        spread = jnp.where(even, gate / (1.0 + jnp.exp(-gate)) * up, 0.0).astype(jnp.bfloat16)
+        act = jnp.dot(spread, select[...], preferred_element_type=jnp.float32)
+        act = act.astype(jnp.bfloat16)
         extra = rows_ref[planes, :, width:].reshape(128, EXTRA).astype(jnp.float32)
         lane = lax.broadcasted_iota(jnp.int32, (128, EXTRA), 1)
         own = (lane == me // 2) | (lane == experts + me // 2)
@@ -219,9 +245,39 @@
         if dz:
             hand_over(block, from_z, dz - 1, 27 + dz, z_near[dz])
 
+    def attend(first, last):
+        for row in range(first, last):
+            keys = cache_latent[row]
+            scores = lax.dot_general(
+                query_latent[row],
+                keys,
+                (((1,), (1,)), ((), ())),
+                preferred_element_type=jnp.float32,
+            )
+            scores += jnp.dot(
+                query_rope[row], cache_rope[row], preferred_element_type=jnp.float32
+            )
+            scores *= 1.0 / math.sqrt(NOPE + ROPE)
+            live = lax.broadcasted_iota(jnp.int32, scores.shape, 1) < lengths_ref[row]
+            scores = jnp.where(live, scores, -1e30)
+            top = jnp.max(scores, axis=1, keepdims=True)
+            raw = jnp.where(live, jnp.exp(scores - top), 0.0)
+            probs = (raw / jnp.sum(raw, axis=1, keepdims=True)).astype(jnp.bfloat16)
+            attn_ref[row] = jnp.dot(probs, keys, preferred_element_type=jnp.float32).astype(
+                jnp.bfloat16
+            )
+
+    quarter = attn_ref.shape[0] // 4
     gather_first(0)
+    wide = lax.broadcasted_iota(jnp.int32, select.shape, 0)
+    narrow = lax.broadcasted_iota(jnp.int32, select.shape, 1)
+    select[...] = jnp.where(wide == 2 * narrow, 1.0, 0.0).astype(jnp.bfloat16)
+    for copy in attn_copies:
+        copy.wait()
+    attend(0, quarter)
     gather_first(1)
     gather_second(0)
+    attend(quarter, 2 * quarter)
     gather_first(2)
     gather_second(1)
     gather_last(0)
@@ -242,9 +298,11 @@
     sum_q(1)
     sum_p(0)
     compute(3)
+    attend(2 * quarter, 3 * quarter)
     sum_cores(3)
     sum_q(2)
     sum_p(1)
+    attend(3 * quarter, 4 * quarter)
     sum_q(3)
     sum_p(2)
     sum_p(3)
@@ -257,7 +315,7 @@
         copy.wait_send()
 
 
-def experts_layer(own, gate_up, down):
+def experts_layer(lengths, own, gate_up, down, *attention):
     hidden_dev, width = down.shape
     rows_dev = own.shape[0]
     groups = lax.axis_size("exp")
@@ -265,60 +323,45 @@
     flops = 2 * groups * rows_dev * width * hidden_dev * 3
     return pl.pallas_call(
         expert_kernel,
-        out_shape=jax.ShapeDtypeStruct(block, jnp.bfloat16),
+        out_shape=(
+            jax.ShapeDtypeStruct(block, jnp.bfloat16),
+            jax.ShapeDtypeStruct(attention[0].shape, jnp.bfloat16),
+        ),
         in_specs=[
+            pl.BlockSpec(memory_space=pltpu.SMEM),
             pl.BlockSpec(memory_space=pltpu.VMEM),
-            pl.BlockSpec(memory_space=pl.ANY),
-            pl.BlockSpec(memory_space=pl.ANY),
+            *([pl.BlockSpec(memory_space=pl.ANY)] * 6),
         ],
-        out_specs=pl.BlockSpec(memory_space=pltpu.VMEM),
+        out_specs=(
+            pl.BlockSpec(memory_space=pltpu.VMEM),
+            pl.BlockSpec(memory_space=pltpu.VMEM),
+        ),
         scratch_shapes=[
             pltpu.VMEM((groups, rows_dev, width + EXTRA), jnp.bfloat16),
-            pltpu.VMEM((2, hidden_dev, width), jnp.bfloat16),
+            pltpu.VMEM((2 * hidden_dev, width), jnp.bfloat16),
             pltpu.VMEM((hidden_dev, width), jnp.bfloat16),
             pltpu.VMEM((groups, *block), jnp.bfloat16),
             pltpu.VMEM((16, *block), jnp.bfloat16),
             pltpu.VMEM((8, *block), jnp.bfloat16),
             pltpu.VMEM((4, *block), jnp.bfloat16),
             pltpu.VMEM((3, *block), jnp.bfloat16),
-            pltpu.VMEM((8 * rows_dev, hidden_dev), jnp.float32),
-            pltpu.VMEM((8 * rows_dev, hidden_dev), jnp.float32),
+            pltpu.VMEM((8 * rows_dev, 2 * hidden_dev), jnp.float32),
+            pltpu.VMEM((2 * hidden_dev, hidden_dev), jnp.bfloat16),
+            *[pltpu.VMEM(array.shape, array.dtype) for array in attention],
             pltpu.SemaphoreType.DMA((2,)),
+            pltpu.SemaphoreType.DMA((4,)),
             pltpu.SemaphoreType.DMA((31,)),
             pltpu.SemaphoreType.DMA((groups,)),
             pltpu.SemaphoreType.DMA((31,)),
             pltpu.SemaphoreType.DMA((31,)),
         ],
         compiler_params=pltpu.CompilerParams(
-            collective_id=0, has_side_effects=True, vmem_limit_bytes=56 * 2**20
+            collective_id=0, has_side_effects=True, vmem_limit_bytes=60 * 2**20
         ),
         cost_estimate=pl.CostEstimate(
             flops=flops, bytes_accessed=6 * hidden_dev * width, transcendentals=0
         ),
-    )(own, gate_up, down)
-
-
-def attend(query_latent, query_rope, cache_latent, cache_rope, row_lengths):
-    score_scale = 1.0 / math.sqrt(NOPE + ROPE)
-    scores = jnp.einsum(
-        "rhc,rlc->rhl", query_latent, cache_latent, preferred_element_type=jnp.float32
-    )
-    scores = scores + jnp.einsum(
-        "rhp,rpl->rhl", query_rope, cache_rope, preferred_element_type=jnp.float32
-    )
-    scores = scores * score_scale
-    valid_mask = (
-        jnp.arange(cache_latent.shape[1], dtype=jnp.int32)[None, None, :]
-        < row_lengths[:, None, None]
-    )
-    scores = jnp.where(valid_mask, scores, -1e30)
-    row_max = jnp.max(scores, axis=2, keepdims=True)
-    weights_raw = jnp.where(valid_mask, jnp.exp(scores - row_max), 0.0)
-    attn_probs = (weights_raw / jnp.sum(weights_raw, axis=2, keepdims=True)).astype(jnp.bfloat16)
-    output = jnp.einsum(
-        "rhl,rlc->rhc", attn_probs, cache_latent, preferred_element_type=jnp.float32
-    )
-    return output.astype(jnp.bfloat16)
+    )(lengths, own, gate_up, down, *attention)
 
 
 def on_device(
@@ -353,8 +396,16 @@
     extra = jnp.concatenate((high, dense_mixing - high), axis=1)
     extra = jnp.pad(extra, ((0, 0), (0, EXTRA - extra.shape[1]))).astype(jnp.bfloat16)
     own = jnp.concatenate((hidden, extra), axis=1)
-    moe_out = experts_layer(own, slice_gate_up.transpose(1, 0, 2), slice_down)
-    attn_latent = attend(query_latent, query_rope, cache_latent, cache_rope, lengths)
+    moe_out, attn_latent = experts_layer(
+        lengths,
+        own,
+        slice_gate_up,
+        slice_down,
+        query_latent,
+        query_rope,
+        cache_latent,
+        cache_rope,
+    )
     return (moe_out, attn_latent)
 
 

time: 130 us -> 112 us (0.86)
  the two profiles are of different devices: /device:TPU:17 before, /device:TPU:0 now
where the time goes in v3:
time: 112 us; the launch traced here: 111 us
  Pallas kernels  102 us (91%)
  local copies, waits for them, and re-layouts  5.02 us (4%)
  other arithmetic  2.07 us (2%)
  matrix products  1.13 us (1%)
    pallas_call x1, Pallas kernels, experts_layer(): pl.pallas_call(expert_kernel, out_shape=(jax.ShapeDtypeStruct(block, jnp....  102 us
    unnamed x5, local copies, waits for them, and re-layouts  4.88 us

profile of v3, /device:TPU:0, one launch (start us, length us, event | category | flops | bytes accessed | tf_op | source)
XLA Modules:
  0.0 110.7 jit_solution(11666989022997567057)
XLA Ops:
  0.6 0.0 copy-start
  0.6 0.8 copy.15
  1.4 0.1 copy-done
  1.6 1.1 %fusion.4 = f32[16,16]{1,0:T(8,128)S(1)} fusion(bf16[16,7168]{1,0:T(8,128)(2,1)} %param.10, bf16[7168,16]{0,1:T(8,128)(2,1)S(1)} %copy-done), kind=kOutput, calls=%fused_computation.14 | convolution fusion | flops 3670016 | bytes 459776 | tf_op jit(solution)/shard_map/dot_general | solution.py:387
  2.7 0.2 select_reduce_fusion.1
  2.9 0.1 copy.16
  3.0 0.1 copy.17
  3.1 0.1 select_reduce_fusion
  3.2 0.1 fusion.3
  3.3 1.6 %pad_maximum_fusion.own_ref = bf16[16,7296]{1,0:T(8,128)(2,1)} fusion(bf16[16,128]{1,0:T(8,128)(2,1)S(1)} %fusion.3, bf16[16,7168]{1,0:T(8,128)(2,1)} %param.10), kind=kLoop, calls=%fused_computation | loop fusion | flops 466944 | bytes 466944 | tf_op jit(solution)/shard_map/concatenate | solution.py:398
  5.0 101.8 %shard_map.113 = (bf16[16,7168]{1,0:T(8,128)(2,1)}, bf16[16,64,512]{2,1,0:T(8,128)(2,1)}) custom-call(s32[16]{0:T(128)} %lengths_ref.1, bf16[16,7296]{1,0:T(8,128)(2,1)} %pad_maximum_fusion.own_ref, bf16[512,2,7168]{2,1,0:T(2,128)(2,1)} %bitcast.4, bf16[512,7168]{1,0:T(8,128)(2,1)} %bitcast.5, bf16[16,64,512]{2,1,0:T(8,128)(2,1)} %query_latent_hbm.1, ...), custom_call_target="tpu_custom_call" | custom-call | flops 11274289152 | bytes 22020096 | tf_op jit(solution)/shard_map/pallas_call | solution.py:324
  106.7 1.6 %copy.20 = bf16[16,7168]{1,0:T(8,128)(2,1)} copy(bf16[16,7168]{1,0:T(8,128)(2,1)} %get-tuple-element.6) | data formatting | bytes 458752
  108.4 2.3 %copy.21 = bf16[16,64,512]{2,1,0:T(8,128)(2,1)} copy(bf16[16,64,512]{2,1,0:T(8,128)(2,1)} %get-tuple-element.7) | data formatting | bytes 2097152
  (3 shorter events, 0.0 us)
Async XLA Ops:
  0.6 1.0 copy-start

commit v4 on v3

--- a/solution.py
+++ b/solution.py
@@ -41,6 +41,7 @@
     from_p,
     from_z,
     acc,
+    act_ref,
     select,
     query_latent,
     query_rope,
@@ -176,16 +177,16 @@
         total = part_ref[block].astype(jnp.float32) + slots[slot].astype(jnp.float32)
         part_ref[block] = total.astype(jnp.bfloat16)
 
-    def compute(dz):
-        zz = other_z(z, dz)
+    def hidden_units(pair):
+        half = z // 2 if pair == 0 else 1 - z // 2
+        planes = pl.ds(16 * half, 16)
         acc[...] = jnp.zeros_like(acc)
         dims = (((1,), (1,)), ((), ()))
-        planes = pl.ds(8 * zz, 8)
 
         @pl.loop(0, width // tile)
         def _(step):
             columns = pl.ds(pl.multiple_of(step * tile, tile), tile)
-            rows = rows_ref[planes, :, columns].reshape(128, tile)
+            rows = rows_ref[planes, :, columns].reshape(256, tile)
             acc[...] += lax.dot_general(
                 rows, gate_up_ref[:, columns], dims, preferred_element_type=jnp.float32
             )
@@ -195,7 +196,12 @@
         even = lax.broadcasted_iota(jnp.int32, gate.shape, 1) % 2 == 0
         spread = jnp.where(even, gate / (1.0 + jnp.exp(-gate)) * up, 0.0).astype(jnp.bfloat16)
         act = jnp.dot(spread, select[...], preferred_element_type=jnp.float32)
-        act = act.astype(jnp.bfloat16)
+        act_ref[pl.ds(pl.multiple_of(256 * half, 256), 256), :] = act.astype(jnp.bfloat16)
+
+    def outputs(dz):
+        zz = other_z(z, dz)
+        planes = pl.ds(8 * zz, 8)
+        act = act_ref[pl.ds(pl.multiple_of(128 * zz, 128), 128), :]
         extra = rows_ref[planes, :, width:].reshape(128, EXTRA).astype(jnp.float32)
         lane = lax.broadcasted_iota(jnp.int32, (128, EXTRA), 1)
         own = (lane == me // 2) | (lane == experts + me // 2)
@@ -281,28 +287,30 @@
     gather_first(2)
     gather_second(1)
     gather_last(0)
-    gate_up_copy.wait()
-    compute(0)
     gather_first(3)
     gather_second(2)
+    attend(2 * quarter, 3 * quarter)
     gather_last(1)
+    gather_second(3)
+    gate_up_copy.wait()
+    hidden_units(0)
+    outputs(0)
+    gather_last(2)
+    outputs(1)
     sum_cores(0)
-    compute(1)
-    gather_second(3)
-    gather_last(2)
+    gather_last(3)
+    hidden_units(1)
     sum_cores(1)
     sum_q(0)
-    compute(2)
-    gather_last(3)
-    sum_cores(2)
+    outputs(2)
     sum_q(1)
     sum_p(0)
-    compute(3)
-    attend(2 * quarter, 3 * quarter)
+    outputs(3)
+    sum_cores(2)
+    sum_p(1)
+    attend(3 * quarter, 4 * quarter)
     sum_cores(3)
     sum_q(2)
-    sum_p(1)
-    attend(3 * quarter, 4 * quarter)
     sum_q(3)
     sum_p(2)
     sum_p(3)
@@ -345,7 +353,8 @@
             pltpu.VMEM((8, *block), jnp.bfloat16),
             pltpu.VMEM((4, *block), jnp.bfloat16),
             pltpu.VMEM((3, *block), jnp.bfloat16),
-            pltpu.VMEM((8 * rows_dev, 2 * hidden_dev), jnp.float32),
+            pltpu.VMEM((16 * rows_dev, 2 * hidden_dev), jnp.float32),
+            pltpu.VMEM((groups * rows_dev, hidden_dev), jnp.bfloat16),
             pltpu.VMEM((2 * hidden_dev, hidden_dev), jnp.bfloat16),
             *[pltpu.VMEM(array.shape, array.dtype) for array in attention],
             pltpu.SemaphoreType.DMA((2,)),

time: 112 us -> 113 us (level)
  Pallas kernels: 102 us -> 104 us
    pallas_call x1, Pallas kernels: 102 us -> 104 us  [experts_layer(): pl.pallas_call(expert_kernel, out_shape=(jax.ShapeDtypeStruct(block, jnp....]
where the time goes in v4:
time: 113 us
  Pallas kernels  104 us (92%)
  local copies, waits for them, and re-layouts  5.02 us (4%)
  other arithmetic  2.07 us (2%)
    pallas_call x1, Pallas kernels, experts_layer(): pl.pallas_call(expert_kernel, out_shape=(jax.ShapeDtypeStruct(block, jnp....  104 us
    unnamed x5, local copies, waits for them, and re-layouts  4.88 us

profile of v4, /device:TPU:0, one launch (start us, length us, event | category | flops | bytes accessed | tf_op | source)
XLA Modules:
  0.0 112.6 jit_solution(11310791089290929743)
XLA Ops:
  0.6 0.0 copy-start
  0.6 0.8 copy.15
  1.4 0.1 copy-done
  1.6 1.1 %fusion.4 = f32[16,16]{1,0:T(8,128)S(1)} fusion(bf16[16,7168]{1,0:T(8,128)(2,1)} %param.10, bf16[7168,16]{0,1:T(8,128)(2,1)S(1)} %copy-done), kind=kOutput, calls=%fused_computation.14 | convolution fusion | flops 3670016 | bytes 459776 | tf_op jit(solution)/shard_map/dot_general | solution.py:396
  2.7 0.2 select_reduce_fusion.1
  2.9 0.1 copy.16
  3.0 0.1 copy.17
  3.1 0.1 select_reduce_fusion
  3.2 0.1 fusion.3
  3.3 1.6 %pad_maximum_fusion.own_ref = bf16[16,7296]{1,0:T(8,128)(2,1)} fusion(bf16[16,128]{1,0:T(8,128)(2,1)S(1)} %fusion.3, bf16[16,7168]{1,0:T(8,128)(2,1)} %param.10), kind=kLoop, calls=%fused_computation | loop fusion | flops 466944 | bytes 466944 | tf_op jit(solution)/shard_map/concatenate | solution.py:407
  5.0 103.7 %shard_map.113 = (bf16[16,7168]{1,0:T(8,128)(2,1)}, bf16[16,64,512]{2,1,0:T(8,128)(2,1)}) custom-call(s32[16]{0:T(128)} %lengths_ref.1, bf16[16,7296]{1,0:T(8,128)(2,1)} %pad_maximum_fusion.own_ref, bf16[512,2,7168]{2,1,0:T(2,128)(2,1)} %bitcast.4, bf16[512,7168]{1,0:T(8,128)(2,1)} %bitcast.5, bf16[16,64,512]{2,1,0:T(8,128)(2,1)} %query_latent_hbm.1, ...), custom_call_target="tpu_custom_call" | custom-call | flops 11274289152 | bytes 22020096 | tf_op jit(solution)/shard_map/pallas_call | solution.py:332
  108.6 1.6 %copy.20 = bf16[16,7168]{1,0:T(8,128)(2,1)} copy(bf16[16,7168]{1,0:T(8,128)(2,1)} %get-tuple-element.6) | data formatting | bytes 458752
  110.3 2.3 %copy.21 = bf16[16,64,512]{2,1,0:T(8,128)(2,1)} copy(bf16[16,64,512]{2,1,0:T(8,128)(2,1)} %get-tuple-element.7) | data formatting | bytes 2097152
  (3 shorter events, 0.0 us)
Async XLA Ops:
  0.6 1.0 copy-start

commit v5 on v3

--- a/solution.py
+++ b/solution.py
@@ -281,14 +281,14 @@
     gather_first(2)
     gather_second(1)
     gather_last(0)
+    gather_first(3)
+    gather_second(2)
     gate_up_copy.wait()
     compute(0)
-    gather_first(3)
-    gather_second(2)
+    gather_second(3)
     gather_last(1)
     sum_cores(0)
     compute(1)
-    gather_second(3)
     gather_last(2)
     sum_cores(1)
     sum_q(0)

time: 112 us -> 114 us (1.018)
  Pallas kernels: 102 us -> 104 us
    pallas_call x1, Pallas kernels: 102 us -> 104 us  [experts_layer(): pl.pallas_call(expert_kernel, out_shape=(jax.ShapeDtypeStruct(block, jnp....]
where the time goes in v5:
time: 114 us; the launch traced here: 113 us
  Pallas kernels  104 us (91%)
  local copies, waits for them, and re-layouts  5.02 us (4%)
  other arithmetic  2.07 us (2%)
    pallas_call x1, Pallas kernels, experts_layer(): pl.pallas_call(expert_kernel, out_shape=(jax.ShapeDtypeStruct(block, jnp....  104 us
    unnamed x5, local copies, waits for them, and re-layouts  4.88 us

profile of v5, /device:TPU:0, one launch (start us, length us, event | category | flops | bytes accessed | tf_op | source)
XLA Modules:
  0.0 113.0 jit_solution(9378339710593540461)
XLA Ops:
  0.6 0.0 copy-start
  0.6 0.8 copy.15
  1.4 0.1 copy-done
  1.6 1.1 %fusion.4 = f32[16,16]{1,0:T(8,128)S(1)} fusion(bf16[16,7168]{1,0:T(8,128)(2,1)} %param.10, bf16[7168,16]{0,1:T(8,128)(2,1)S(1)} %copy-done), kind=kOutput, calls=%fused_computation.14 | convolution fusion | flops 3670016 | bytes 459776 | tf_op jit(solution)/shard_map/dot_general | solution.py:387
  2.7 0.2 select_reduce_fusion.1
  2.9 0.1 copy.16
  3.0 0.1 copy.17
  3.1 0.1 select_reduce_fusion
  3.2 0.1 fusion.3
  3.3 1.6 %pad_maximum_fusion.own_ref = bf16[16,7296]{1,0:T(8,128)(2,1)} fusion(bf16[16,128]{1,0:T(8,128)(2,1)S(1)} %fusion.3, bf16[16,7168]{1,0:T(8,128)(2,1)} %param.10), kind=kLoop, calls=%fused_computation | loop fusion | flops 466944 | bytes 466944 | tf_op jit(solution)/shard_map/concatenate | solution.py:398
  5.0 104.1 %shard_map.113 = (bf16[16,7168]{1,0:T(8,128)(2,1)}, bf16[16,64,512]{2,1,0:T(8,128)(2,1)}) custom-call(s32[16]{0:T(128)} %lengths_ref.1, bf16[16,7296]{1,0:T(8,128)(2,1)} %pad_maximum_fusion.own_ref, bf16[512,2,7168]{2,1,0:T(2,128)(2,1)} %bitcast.4, bf16[512,7168]{1,0:T(8,128)(2,1)} %bitcast.5, bf16[16,64,512]{2,1,0:T(8,128)(2,1)} %query_latent_hbm.1, ...), custom_call_target="tpu_custom_call" | custom-call | flops 11274289152 | bytes 22020096 | tf_op jit(solution)/shard_map/pallas_call | solution.py:324
  109.0 1.6 %copy.20 = bf16[16,7168]{1,0:T(8,128)(2,1)} copy(bf16[16,7168]{1,0:T(8,128)(2,1)} %get-tuple-element.6) | data formatting | bytes 458752
  110.7 2.3 %copy.21 = bf16[16,64,512]{2,1,0:T(8,128)(2,1)} copy(bf16[16,64,512]{2,1,0:T(8,128)(2,1)} %get-tuple-element.7) | data formatting | bytes 2097152
  (3 shorter events, 0.0 us)
Async XLA Ops:
  0.6 1.0 copy-start
